TPU v7x, 512 devices: a whole 4x4x16 slice. The times are simulated.
512 devices in a mesh: rep: 32 (over y, x, core), seq: 16 (over z).
Axes of the slice: x: 4, y: 4, z: 16, core: 2. Of those that a mesh axis runs over, the one named last changes fastest.
Arguments:
- queries: bfloat16 [8192, 24576], P(('rep', 'seq')), parts along dimension 0, may hold values from -64 to 64
- stretch_latent: bfloat16 [8192, 576], P(('rep', 'seq')), parts along dimension 0, may hold values from -6 to 6
- prefix_latent: bfloat16 [57344, 576], P(('rep', 'seq')), parts along dimension 0, may hold values from -6 to 6
- kv_up_weight: bfloat16 [512, 32768], P(None, 'seq'), may hold values from -0.25 to 0.25
Outputs:
- attended: bfloat16 [8192, 16384], P(('rep', 'seq')), parts along dimension 0
There are 32 independent parts, one for each index of `rep`. A program takes and returns all parts, laid end to end along the dimension named above; an argument that names none is the same for every part. Nothing has to cross between parts.
All inputs are finite; a program needn't handle non-finite values.
Results may differ from a plain program's by a relative error of at most 0.0073.
Values may be sent and summed in bfloat16 or wider, within the bound.
A program may use at most 64 MiB of HBM per device.

v0:
```python
import math

import jax
import jax.numpy as jnp
from jax import lax
from jax.sharding import PartitionSpec as P

KV_RANK = 512
ROPE = 64
NOPE = 128
VDIM = 128


def dot_rows(left, right):
    return lax.dot_general(
        left, right, (((1,), (1,)), ((), ())), preferred_element_type=jnp.float32
    )


def head_attention(q_head, head_kv, rope_keys, prefix_len):
    score_scale = 1.0 / math.sqrt(NOPE + ROPE)
    q_nope = q_head[:, :NOPE]
    q_rope = q_head[:, NOPE:]
    key_nope = head_kv[:, :NOPE]
    values = head_kv[:, NOPE:]
    scores = (dot_rows(q_nope, key_nope) + dot_rows(q_rope, rope_keys)) * score_scale
    row_index = lax.broadcasted_iota(jnp.int32, scores.shape, 0)
    col_index = lax.broadcasted_iota(jnp.int32, scores.shape, 1)
    visible = col_index <= row_index + prefix_len
    scores = jnp.where(visible, scores, -jnp.inf)
    row_max = jnp.max(scores, axis=1, keepdims=True)
    exponent = jnp.where(visible, jnp.exp(scores - row_max), 0.0)
    weights = (exponent / jnp.sum(exponent, axis=1, keepdims=True)).astype(jnp.bfloat16)
    return jnp.dot(weights, values, preferred_element_type=jnp.float32).astype(jnp.bfloat16)


def return_rows(holder):
    return lax.all_to_all(holder, "seq", split_axis=0, concat_axis=1, tiled=True)


def body(queries, stretch_latent, prefix_latent, kv_up_weight):
    query_width = NOPE + ROPE
    head_span = NOPE + VDIM
    head_count = kv_up_weight.shape[1] // head_span
    seq_count = lax.axis_size("seq")
    prefix_len = prefix_latent.shape[0] * seq_count
    stretch_total = queries.shape[0] * seq_count
    prefix_all, stretch_all = (
        lax.all_gather(prefix_latent, "seq", axis=0, tiled=True),
        lax.all_gather(stretch_latent, "seq", axis=0, tiled=True),
    )
    all_latent = jnp.concatenate([prefix_all, stretch_all], axis=0)
    rope_keys = all_latent[:, KV_RANK:]
    latent_part = all_latent[:, :KV_RANK]

    def head_keys(head_index):
        weight_cols = lax.dynamic_slice_in_dim(kv_up_weight, head_index * head_span, head_span, 1)
        return jnp.dot(latent_part, weight_cols, preferred_element_type=jnp.float32).astype(
            jnp.bfloat16
        )

    local_queries = lax.all_to_all(queries, "seq", split_axis=1, concat_axis=0, tiled=True)

    def attend(head_index):
        q_head = lax.dynamic_slice_in_dim(local_queries, head_index * query_width, query_width, 1)
        return head_attention(q_head, head_keys(head_index), rope_keys, prefix_len)

    def fill_head(head_index, holder):
        return lax.dynamic_update_slice_in_dim(holder, attend(head_index), head_index * VDIM, 1)

    holder = lax.fori_loop(
        0, head_count, fill_head, jnp.zeros((stretch_total, head_count * VDIM), jnp.bfloat16)
    )
    return return_rows(holder)


def solution(mesh):
    in_specs = (
        P(("rep", "seq"), None),
        P(("rep", "seq"), None),
        P(("rep", "seq"), None),
        P(None, "seq"),
    )
    out_specs = P(("rep", "seq"), None)
    return jax.shard_map(body, mesh=mesh, in_specs=in_specs, out_specs=out_specs, check_vma=False)
```

profile of v0, /device:TPU:22, one launch (start us, length us, event | category | flops | bytes accessed | tf_op | source)
XLA Modules:
  0.0 189.5 jit_solution(8358021939840637296)
XLA Ops:
  6.5 0.0 copy-start
  6.5 0.0 all-gather.2.cloned.1.call-start
  6.5 0.7 all-gather.2.cloned.1.call-update
  7.3 2.1 %copy.13 = bf16[2,16,8,1536]{3,2,0,1:T(8,128)(2,1)} copy(bf16[2,16,8,1536]{3,2,1,0:T(8,128)(2,1)} %bitcast.24) | data formatting | bytes 1572864 | tf_op jit(solution)/shard_map/all_to_all | solution.py:62
  9.4 15.2 %all-to-all-start = ((bf16[16,16,1536]{2,0,1:T(8,128)(2,1)}), bf16[16,16,1536]{2,0,1:T(8,128)(2,1)S(1)}, u32[]{:S(2)}, u32[]{:S(2)}) async-start(bf16[16,16,1536]{2,0,1:T(8,128)(2,1)} %bitcast.14), calls=%async_computation | async-start | bytes 1572864 | tf_op jit(solution)/shard_map/all_to_all | solution.py:62
  24.6 0.0 copy-done
  24.6 70.4 %all_gather.7 = bf16[256,576]{1,0:T(8,128)(2,1)S(1)} all-gather(bf16[16,576]{1,0:T(8,128)(2,1)S(1)} %copy-done), channel_id=1, replica_groups=mesh['rep'=32,'seq'=16] {'seq'}, dimensions={0}, use_global_device_ids=true | all-gather | bytes 313344 | tf_op jit(solution)/shard_map/all_gather | solution.py:50
  95.0 13.8 %all-gather.2.cloned.1.call-done = bf16[1792,576]{1,0:T(8,128)(2,1)} async-done(((bf16[112,576]{1,0:T(8,128)(2,1)}), bf16[1792,576]{1,0:T(8,128)(2,1)}) %all-gather.2.cloned.1.call-update) | async-done | bytes 2064400 | tf_op jit(solution)/shard_map/all_gather | solution.py:49
  108.8 1.8 constant_dynamic-update-slice_fusion.1
  110.7 0.2 slice.38
  110.9 0.0 all-to-all-done
  110.9 0.9 broadcast_in_dim.24
  111.8 39.5 %while.13 = (s32[]{:T(128)}, bf16[256,1024]{1,0:T(8,128)(2,1)}, bf16[256,1536]{1,0:T(8,128)(2,1)S(1)}, bf16[512,2048]{1,0:T(8,128)(2,1)}, bf16[2048,512]{1,0:T(8...) while((s32[]{:T(128)}, bf16[256,1024]{1,0:T(8,128)(2,1)}, ...), condition=%wide.region_3.4_spmd, body=%wide.region_0.3_spmd.sunk | while | flops 880312064 | bytes 15672635 | solution.py:71
  111.8 1.7 fusion.35
  113.5 0.5 fusion.36
  114.0 0.7 fusion.37
  114.7 0.6 fusion.38
  115.3 1.4 fusion.39
  116.7 1.7 fusion.35
  118.4 0.5 fusion.36
  118.9 0.7 fusion.37
  119.7 0.6 fusion.38
  120.3 1.4 fusion.39
  121.7 1.7 fusion.35
  123.4 0.5 fusion.36
  123.9 0.7 fusion.37
  124.6 0.6 fusion.38
  125.2 1.4 fusion.39
  126.6 1.7 fusion.35
  128.3 0.5 fusion.36
  128.8 0.7 fusion.37
  129.5 0.6 fusion.38
  130.2 1.4 fusion.39
  131.5 1.7 fusion.35
  133.3 0.5 fusion.36
  133.8 0.7 fusion.37
  134.5 0.6 fusion.38
  135.1 1.4 fusion.39
  136.5 1.7 fusion.35
  138.2 0.5 fusion.36
  138.7 0.7 fusion.37
  139.4 0.6 fusion.38
  140.1 1.4 fusion.39
  141.4 1.7 fusion.35
  143.1 0.5 fusion.36
  143.6 0.7 fusion.37
  144.4 0.6 fusion.38
  145.0 1.4 fusion.39
  146.4 1.7 fusion.35
  148.1 0.5 fusion.36
  148.6 0.7 fusion.37
  149.3 0.6 fusion.38
  149.9 1.4 fusion.39
  151.3 30.5 %all_to_all.38 = bf16[16,16,1024]{2,1,0:T(8,128)(2,1)S(1)} all-to-all(bf16[16,16,1024]{2,1,0:T(8,128)(2,1)} %bitcast.22), channel_id=1, replica_groups=mesh['rep'=32,'seq'=16] {'seq'}, dimensions={0} | all-to-all | bytes 1048576 | tf_op jit(solution)/shard_map/all_to_all | solution.py:38
  181.8 0.8 copy.11
  (10 shorter events, 0.1 us)
Async XLA Ops:
  6.5 18.0 %copy-start = (bf16[16,576]{1,0:T(8,128)(2,1)S(1)}, bf16[16,576]{1,0:T(8,128)(2,1)}, u32[]{:S(2)}) copy-start(bf16[16,576]{1,0:T(8,128)(2,1)} %param.7) | copy-start | bytes 55300
  6.5 102.3 %all-gather.2.cloned.1.call-start = ((), (), s32[]{:S(2)}) async-start(), calls=%async_computation.2 | async-start | bytes 2437120 | tf_op jit(solution)/shard_map/all_gather | solution.py:49
  9.4 101.5 %all-to-all-start = ((bf16[16,16,1536]{2,0,1:T(8,128)(2,1)}), bf16[16,16,1536]{2,0,1:T(8,128)(2,1)S(1)}, u32[]{:S(2)}, u32[]{:S(2)}) async-start(bf16[16,16,1536]{2,0,1:T(8,128)(2,1)} %bitcast.14), calls=%async_computation | async-start | bytes 1572864 | tf_op jit(solution)/shard_map/all_to_all | solution.py:62
Sparse Core Ops, SparseCore 0:
  9.4 99.3 all-gather.1
where the time goes:
time: 190 us; the launch traced here: 189 us
  blocking collectives  101 us (53%)
  matrix products  34.4 us (18%)
  starting transfers between devices  15.2 us (8%)
  waiting for transfers between devices  14.5 us (8%)
  between operations  13.4 us (7%)
  local copies, waits for them, and re-layouts  5.89 us (3%)
  other arithmetic  5.02 us (3%)
    all_gather x1, blocking collectives, body(): lax.all_gather(stretch_latent, 'seq', axis=0, tiled=True)  70.4 us
    all_to_all x1, blocking collectives, return_rows(): lax.all_to_all(holder, 'seq', split_axis=0, concat_axis=1, tiled=True)  30.5 us
    all_to_all x1, starting transfers between devices, body(): lax.all_to_all(queries, 'seq', split_axis=1, concat_axis=0, tiled=True)  15.2 us
    all_gather x1, waiting for transfers between devices, body(): lax.all_gather(prefix_latent, 'seq', axis=0, tiled=True)  13.8 us
    dot_general x8, matrix products, head_keys(): jnp.dot(latent_part, weight_cols, preferred_element_type=jnp.float32)  13.7 us
    dot_general x8, matrix products, head_attention(): jnp.dot(weights, values, preferred_element_type=jnp.float32)  11 us
    dot_general x16, matrix products, dot_rows(): lax.dot_general(left, right, (((1,), (1,)), ((), ())), preferred_element_...  9.82 us
    reduce_sum x8, other arithmetic, head_attention(): jnp.sum(exponent, axis=1, keepdims=True)  5 us
  transfers between devices with their start and end apart: 2, of which 1 were waited for; matrix products, arithmetic and copies ran while one was open for 2% of the time, Pallas kernels for 0%

commit v1 on v0

v1 whole, which is shorter than its diff:
```python
import functools
import math

import jax
import jax.numpy as jnp
from jax import lax
from jax.experimental import pallas as pl
from jax.experimental.pallas import tpu as pltpu
from jax.sharding import PartitionSpec as P

KV_RANK = 512
ROPE = 64
NOPE = 128
VDIM = 128
QW = NOPE + ROPE
SPAN = NOPE + VDIM
SEQ = 16
HEADS_HERE = 8
PRE = 112
NEW = 16
KEYS = SEQ * (PRE + NEW)
PRE_ALL = SEQ * PRE
WINDOW = 8
ROWS = WINDOW * NEW
CHUNK = 144
SUB = 48
MESH = pl.DeviceIdType.MESH
BF = jnp.bfloat16
F32 = jnp.float32


def mm(a, b):
    return jnp.dot(a, b, preferred_element_type=F32)


def mm_t(a, b):
    return lax.dot_general(a, b, (((1,), (1,)), ((), ())), preferred_element_type=F32)


def kernel(
    reps, prefix, stretch, q_hbm, w_hbm, out_hbm,
    lat, qbuf, wbuf, kbuf, vbuf, ropes, obuf, perm, sel, bias,
    ring_s, ring_r, q_s, q_r, o_s, o_r, w1_s, w1_r, w2_s, w2_r, loc_w, loc_q, loc_o,
):
    me = lax.axis_index("seq")
    rep = lax.axis_index("rep")
    odd = lax.rem(me, 2)
    slice_rows = KV_RANK // reps

    def at(d):
        return lax.rem(me + d + 2 * SEQ, SEQ)

    def first_of(z):
        return -3 - lax.rem(z, 2)

    own_w = pltpu.make_async_copy(w_hbm, wbuf.at[0], loc_w)
    own_w.start()

    lat[me, 0:PRE, :] = prefix[:, 0:KV_RANK]
    lat[me, PRE : PRE + NEW, :] = stretch[:, 0:KV_RANK]
    r64 = lax.broadcasted_iota(jnp.int32, (ROPE, 128), 0)
    c64 = lax.broadcasted_iota(jnp.int32, (ROPE, 128), 1)
    put_low = jnp.where(c64 == r64, 1.0, 0.0).astype(BF)
    put_high = jnp.where(c64 == r64 + ROPE, 1.0, 0.0).astype(BF)
    for t in range(4):
        low = prefix[32 * t : 32 * t + 16, KV_RANK:]
        high = prefix[32 * t + 16 : 32 * t + 32, KV_RANK:] if t < 3 else stretch[:, KV_RANK:]
        lat[me, 128:CHUNK, 128 * t : 128 * t + 128] = (mm(low, put_low) + mm(high, put_high)).astype(BF)

    barrier = pltpu.get_barrier_semaphore()
    z_partners = (1, -1, 2, -2, 3, -3, 4, -4, 8)
    for d in z_partners:
        pl.semaphore_signal(barrier, inc=1, device_id={"seq": at(d)}, device_id_type=MESH)

    def greet(d, c):
        pl.semaphore_signal(barrier, inc=1, device_id={"rep": lax.rem(rep + d, reps)}, device_id_type=MESH)
        return c

    lax.fori_loop(1, reps, greet, 0)
    pl.semaphore_wait(barrier, len(z_partners) + reps - 1)

    my_slice = pl.ds(pl.multiple_of(rep * slice_rows, 16), slice_rows)
    far_w = pltpu.make_async_remote_copy(
        w_hbm.at[my_slice, :], wbuf.at[1, my_slice, :], w1_s, w1_r, device_id={"seq": at(8)}, device_id_type=MESH
    )
    far_w.start()

    def ring(way, step, rows, j):
        held = at(-step) if way == 0 else at(step)
        ref = lat.at[held, rows]
        return pltpu.make_async_remote_copy(
            ref, ref, ring_s.at[way, step, j], ring_r.at[way, step, j],
            device_id={"seq": at(1) if way == 0 else at(-1)}, device_id_type=MESH,
        )

    def ring_in(way, step, rows, j):
        held = at(-step - 1) if way == 0 else at(step + 1)
        ref = lat.at[held, rows]
        return pltpu.make_async_remote_copy(
            ref, ref, ring_s.at[way, step, j], ring_r.at[way, step, j],
            device_id={"seq": at(1) if way == 0 else at(-1)}, device_id_type=MESH,
        )

    subs = [pl.ds(j * SUB, SUB) for j in range(3)]
    halves = [pl.ds(0, 80), pl.ds(80, 64)]
    for j in range(3):
        for way in (0, 1):
            ring(way, 0, subs[j], j).start()

    def q_copy(shard, d):
        z = at(d)
        head_shard = lax.rem(z + 8 * shard, SEQ)
        slot = -d - first_of(z)
        return pltpu.make_async_remote_copy(
            q_hbm.at[:, pl.ds(pl.multiple_of(head_shard * (HEADS_HERE * QW), 128), HEADS_HERE * QW)],
            qbuf.at[shard, pl.ds(pl.multiple_of(slot * NEW, 16), NEW), :],
            q_s.at[shard, lax.rem(d + SEQ, SEQ)], q_r.at[shard, lax.rem(d + SEQ, SEQ)],
            device_id={"seq": z}, device_id_type=MESH,
        )

    q_away = (1, -1, 2, -2, 3, -3, 8 * odd - 4)

    def q_start(shard):
        head_shard = lax.rem(me + 8 * shard, SEQ)
        slot = -first_of(me)
        pltpu.make_async_copy(
            q_hbm.at[:, pl.ds(pl.multiple_of(head_shard * (HEADS_HERE * QW), 128), HEADS_HERE * QW)],
            qbuf.at[shard, pl.ds(pl.multiple_of(slot * NEW, 16), NEW), :], loc_q.at[shard],
        ).start()
        for d in q_away:
            q_copy(shard, d).start()

    def q_wait(shard):
        pltpu.make_async_copy(
            q_hbm.at[:, 0 : HEADS_HERE * QW], qbuf.at[shard, 0:NEW, :], loc_q.at[shard]
        ).wait()
        for d in (1, -1, 2, -2, 3, -3, 8 * odd - 4):
            q_copy(shard, d).wait_recv()

    q_start(0)

    far_w.wait_recv()

    def w_copy(d):
        return pltpu.make_async_remote_copy(
            wbuf.at[1, my_slice, :], wbuf.at[1, my_slice, :], w2_s.at[d], w2_r.at[d],
            device_id={"rep": lax.rem(rep + d, reps)}, device_id_type=MESH,
        )

    def spread(d, c):
        w_copy(d).start()
        return c

    lax.fori_loop(1, reps, spread, 0)
    q_start(1)

    pr = lax.broadcasted_iota(jnp.int32, (2 * QW, 512), 0)
    pc = lax.broadcasted_iota(jnp.int32, (2 * QW, 512), 1)
    want = jnp.where(pc < 256, jnp.where(pc < QW, pc, -1), jnp.where(pc < 256 + QW, pc - 256 + QW, -1))
    perm[...] = jnp.where(pr == want, 1.0, 0.0).astype(BF)
    sr = lax.broadcasted_iota(jnp.int32, (128, 256), 0)
    sc = lax.broadcasted_iota(jnp.int32, (128, 256), 1)
    want = jnp.where(sc < 128, jnp.where(sc < ROPE, sc, -1), jnp.where(sc < 128 + ROPE, sc - 128 + ROPE, -1))
    sel[...] = jnp.where(sr == want, 1.0, 0.0).astype(BF)
    row = lax.broadcasted_iota(jnp.int32, (ROWS, SEQ * NEW), 0)
    col = lax.broadcasted_iota(jnp.int32, (ROWS, SEQ * NEW), 1)
    token = row + (me + first_of(me) + SEQ) * NEW
    token = jnp.where(token >= 2 * SEQ * NEW, token - 2 * SEQ * NEW, jnp.where(token >= SEQ * NEW, token - SEQ * NEW, token))
    bias[...] = jnp.where(col <= token, 0.0, -jnp.inf)

    def put(ref, head, src, val):
        ref[head, pl.ds(pl.multiple_of(src * PRE, 16), PRE), :] = val[0:PRE]
        ref[head, pl.ds(pl.multiple_of(PRE_ALL + src * NEW, 16), NEW), :] = val[PRE:]

    def project(shard, srcs, heads):
        x = [lat[s, 0:128, :] for s in srcs]
        x = x[0] if len(x) == 1 else jnp.concatenate(x, axis=0)
        for h in heads:
            kv = mm(x, wbuf[shard, :, SPAN * h : SPAN * h + SPAN]).astype(BF)
            for n, s in enumerate(srcs):
                put(kbuf, shard * HEADS_HERE + h, s, kv[128 * n : 128 * n + 128, 0:NOPE])
                put(vbuf, shard * HEADS_HERE + h, s, kv[128 * n : 128 * n + 128, NOPE:])

    def unpack_rope(src):
        for t in range(4):
            pair = mm(lat[src, 128:CHUNK, 128 * t : 128 * t + 128], sel[...]).astype(BF)
            ropes[pl.ds(pl.multiple_of(src * PRE + 32 * t, 16), 16), :] = pair[:, 0:128]
            high = src * PRE + 32 * t + 16 if t < 3 else PRE_ALL + src * NEW
            ropes[pl.ds(pl.multiple_of(high, 16), 16), :] = pair[:, 128:]

    own_w.wait()
    parts = ((0, 1, 2), (3, 4, 5), (6, 7))

    def ring_step(step, last):
        for j in range(3):
            for way in (0, 1):
                ring_in(way, step - 1, subs[j], j).wait_recv()
                if not last:
                    ring(way, step, subs[j], j).start()
            if last and j == 1:
                ring(0, step, halves[0], 0).start()
            if last and j == 2:
                ring(1, step, halves[1], 0).start()
            srcs = (at(1 - step), at(step - 1))
            project(0, srcs, parts[j])
            if j == 2:
                unpack_rope(srcs[0])
                unpack_rope(srcs[1])

    def loop_step(step, c):
        ring_step(step, False)
        return c

    lax.fori_loop(1, 7, loop_step, 0)
    ring_step(7, True)
    srcs = (at(-7), at(7))
    project(0, srcs, range(HEADS_HERE))
    unpack_rope(srcs[0])
    unpack_rope(srcs[1])
    ring_in(0, 7, halves[0], 0).wait_recv()
    ring_in(1, 7, halves[1], 0).wait_recv()
    project(0, (at(8),), range(HEADS_HERE))
    unpack_rope(at(8))

    factor = math.log2(math.e) / math.sqrt(QW)
    o_away = (1, -1, 2, -2, 3, -3, 4 - 8 * odd)

    def o_copy(shard, pair, d):
        slot = d - first_of(me)
        cols = lax.rem(me + 8 * shard, SEQ) * (HEADS_HERE * VDIM) + pair * (2 * VDIM)
        return pltpu.make_async_remote_copy(
            obuf.at[shard * 4 + pair, pl.ds(pl.multiple_of(slot * NEW, 16), NEW), :],
            out_hbm.at[:, pl.ds(pl.multiple_of(cols, 128), 2 * VDIM)],
            o_s.at[shard, pair, lax.rem(d + SEQ, SEQ)], o_r.at[shard, pair, lax.rem(d + SEQ, SEQ)],
            device_id={"seq": at(d)}, device_id_type=MESH,
        )

    def o_local(shard, pair):
        slot = -first_of(me)
        cols = lax.rem(me + 8 * shard, SEQ) * (HEADS_HERE * VDIM) + pair * (2 * VDIM)
        return pltpu.make_async_copy(
            obuf.at[shard * 4 + pair, pl.ds(pl.multiple_of(slot * NEW, 16), NEW), :],
            out_hbm.at[:, pl.ds(pl.multiple_of(cols, 128), 2 * VDIM)], loc_o.at[shard, pair],
        )

    def attend(shard, pair):
        qp = qbuf[shard, :, pl.ds(pl.multiple_of(pair * (2 * QW), 128), 2 * QW)]
        qp = mm(qp, perm[...]).astype(BF)
        for n in range(2):
            head = shard * HEADS_HERE + 2 * pair + n
            keys = jnp.concatenate([kbuf[head], ropes[...]], axis=1)
            s = mm_t(qp[:, 256 * n : 256 * n + 256], keys)
            s = jnp.concatenate([s[:, 0:PRE_ALL], s[:, PRE_ALL:] + bias[...]], axis=1)
            top = jnp.max(s, axis=1, keepdims=True)
            e = jnp.exp2((s - top) * factor)
            total = jnp.sum(e, axis=1, keepdims=True)
            o = mm(e.astype(BF), vbuf[head]) / total
            obuf[shard * 4 + pair, :, VDIM * n : VDIM * n + VDIM] = o.astype(BF)
        o_local(shard, pair).start()
        for d in o_away:
            o_copy(shard, pair, d).start()

    def attend_all(shard):
        def step(pair, c):
            attend(shard, pair)
            return c

        lax.fori_loop(0, 4, step, 0)

    q_wait(0)
    attend_all(0)

    def w_wait(d, c):
        w_copy(d).wait_recv()
        return c

    lax.fori_loop(1, reps, w_wait, 0)

    def far_project(i, c):
        project(1, (2 * i, 2 * i + 1), range(HEADS_HERE))
        return c

    lax.fori_loop(0, SEQ // 2, far_project, 0)
    q_wait(1)
    attend_all(1)

    for shard in (0, 1):
        for d in q_away:
            q_copy(shard, d).wait_send()

        def o_wait(pair, c):
            o_local(shard, pair).wait()
            for d in o_away:
                o_copy(shard, pair, d).wait_send()
                o_copy(shard, pair, d).wait_recv()
            return c

        lax.fori_loop(0, 4, o_wait, 0)
    far_w.wait_send()

    def w_sent(d, c):
        w_copy(d).wait_send()
        return c

    lax.fori_loop(1, reps, w_sent, 0)

    def ring_sent(step, c):
        for way in (0, 1):
            for j in range(3):
                ring(way, step, subs[j], j).wait_send()
        return c

    lax.fori_loop(0, 7, ring_sent, 0)
    for way in (0, 1):
        ring(way, 7, halves[way], 0).wait_send()


def body(queries, stretch_latent, prefix_latent, kv_up_weight):
    reps = lax.axis_size("rep")
    dma = pltpu.SemaphoreType.DMA
    hbm = pl.BlockSpec(memory_space=pl.ANY)
    vmem = pl.BlockSpec(memory_space=pltpu.VMEM)
    return pl.pallas_call(
        functools.partial(kernel, reps),
        out_shape=jax.ShapeDtypeStruct((NEW, SEQ * HEADS_HERE * VDIM), BF),
        in_specs=[vmem, vmem, hbm, hbm],
        out_specs=hbm,
        scratch_shapes=[
            pltpu.VMEM((SEQ, CHUNK, KV_RANK), BF),
            pltpu.VMEM((2, ROWS, HEADS_HERE * QW), BF),
            pltpu.VMEM((2, KV_RANK, HEADS_HERE * SPAN), BF),
            pltpu.VMEM((2 * HEADS_HERE, KEYS, NOPE), BF),
            pltpu.VMEM((2 * HEADS_HERE, KEYS, VDIM), BF),
            pltpu.VMEM((KEYS, 128), BF),
            pltpu.VMEM((HEADS_HERE, ROWS, 2 * VDIM), BF),
            pltpu.VMEM((2 * QW, 512), BF),
            pltpu.VMEM((128, 256), BF),
            pltpu.VMEM((ROWS, SEQ * NEW), F32),
            dma((2, 8, 3)), dma((2, 8, 3)),
            dma((2, SEQ)), dma((2, SEQ)),
            dma((2, 4, SEQ)), dma((2, 4, SEQ)),
            dma, dma, dma((reps,)), dma((reps,)),
            dma, dma((2,)), dma((2, 4)),
        ],
        compiler_params=pltpu.CompilerParams(
            collective_id=0, has_side_effects=True, vmem_limit_bytes=60 * 1024 * 1024
        ),
        cost_estimate=pl.CostEstimate(flops=13_000_000_000, bytes_accessed=8_000_000, transcendentals=4_200_000),
    )(prefix_latent, stretch_latent, queries, kv_up_weight)


def solution(mesh):
    in_specs = (
        P(("rep", "seq"), None),
        P(("rep", "seq"), None),
        P(("rep", "seq"), None),
        P(None, "seq"),
    )
    out_specs = P(("rep", "seq"), None)
    return jax.shard_map(body, mesh=mesh, in_specs=in_specs, out_specs=out_specs, check_vma=False)
```

time: 190 us -> 101 us (0.53)
  the two profiles are of different devices: /device:TPU:22 before, /device:TPU:16 now
where the time goes in v1:
time: 101 us
  Pallas kernels  99.2 us (98%)
  local copies, waits for them, and re-layouts  1.87 us (2%)
    pallas_call x1, Pallas kernels, body(): pl.pallas_call(functools.partial(kernel, reps), out_shape=jax.ShapeDtypeS...  99.2 us

profile of v1, /device:TPU:16, one launch (start us, length us, event | category | flops | bytes accessed | tf_op | source)
XLA Modules:
  0.0 101.0 jit_solution(15802130591309114093)
XLA Ops:
  0.0 99.2 %shard_map.46 = bf16[16,16384]{1,0:T(8,128)(2,1)} custom-call(bf16[112,576]{1,0:T(8,128)(2,1)} %prefix.1, bf16[16,576]{1,0:T(8,128)(2,1)} %stretch.1, bf16[16,24576]{1,0:T(8,128)(2,1)} %q_hbm.1, bf16[512,2048]{1,0:T(8,128)(2,1)} %w_hbm.1), custom_call_target="tpu_custom_call" | custom-call | flops 12999999488 | bytes 8000000 | tf_op jit(solution)/shard_map/pallas_call | solution.py:323
  99.2 1.9 %copy.6 = bf16[16,16384]{1,0:T(8,128)(2,1)} copy(bf16[16,16384]{1,0:T(8,128)(2,1)} %shard_map.46) | data formatting | bytes 1048576

commit v2 on v1

v2 whole, which is shorter than its diff:
```python
import functools
import math

import jax
import jax.numpy as jnp
from jax import lax
from jax.experimental import pallas as pl
from jax.experimental.pallas import tpu as pltpu
from jax.sharding import PartitionSpec as P

KV_RANK = 512
ROPE = 64
NOPE = 128
VDIM = 128
QW = NOPE + ROPE
SPAN = NOPE + VDIM
SEQ = 16
HEADS_HERE = 8
PRE = 112
NEW = 16
KEYS = SEQ * (PRE + NEW)
PRE_ALL = SEQ * PRE
WINDOW = 8
ROWS = WINDOW * NEW
CHUNK = 144
SUB = 48
HALF_AT = 5
FAR_AT = 6
FAR_UNITS = 6 // (7 - FAR_AT)
Q1_FROM = 5
MESH = pl.DeviceIdType.MESH
BF = jnp.bfloat16
F32 = jnp.float32


def mm(a, b):
    return jnp.dot(a, b, preferred_element_type=F32)


def mm_t(a, b):
    return lax.dot_general(a, b, (((1,), (1,)), ((), ())), preferred_element_type=F32)


def kernel(
    reps, prefix_hbm, stretch_hbm, q_hbm, w_hbm, out_hbm,
    own, lat, qbuf, wbuf, kbuf, vbuf, ropes, obuf, perm, sel, bias,
    ring_s, ring_r, q_s, q_r, o_s, o_r, w1_s, w1_r, w2_s, w2_r, w3_s, w3_r, loc_w, loc_x, loc_q, loc_o,
):
    me = lax.axis_index("seq")
    rep = lax.axis_index("rep")
    odd = lax.rem(me, 2)
    chips = reps // 2
    core = lax.rem(rep, 2)
    sibling = rep + 1 - 2 * core
    slice_rows = KV_RANK // reps

    def at(d):
        return lax.rem(me + d + 2 * SEQ, SEQ)

    def first_of(z):
        return -3 - lax.rem(z, 2)

    barrier = pltpu.get_barrier_semaphore()
    z_partners = (1, -1, 2, -2, 3, -3, 4, -4, 8)
    for d in z_partners:
        pl.semaphore_signal(barrier, inc=1, device_id={"seq": at(d)}, device_id_type=MESH)

    def greet(d, c):
        pl.semaphore_signal(barrier, inc=1, device_id={"rep": lax.rem(rep + 2 * d, reps)}, device_id_type=MESH)
        return c

    lax.fori_loop(1, chips, greet, 0)
    pl.semaphore_signal(barrier, inc=1, device_id={"rep": sibling}, device_id_type=MESH)

    own_prefix = pltpu.make_async_copy(prefix_hbm, own.at[0:PRE, :], loc_x.at[0])
    own_stretch = pltpu.make_async_copy(stretch_hbm, own.at[PRE : PRE + NEW, :], loc_x.at[1])
    own_w = pltpu.make_async_copy(w_hbm, wbuf.at[0], loc_w)
    own_prefix.start()
    own_stretch.start()
    own_w.start()
    r64 = lax.broadcasted_iota(jnp.int32, (ROPE, 128), 0)
    c64 = lax.broadcasted_iota(jnp.int32, (ROPE, 128), 1)
    put_low = jnp.where(c64 == r64, 1.0, 0.0).astype(BF)
    put_high = jnp.where(c64 == r64 + ROPE, 1.0, 0.0).astype(BF)
    own_prefix.wait()
    own_stretch.wait()
    lat[me, 0:128, :] = own[:, 0:KV_RANK]
    low = mm(own[:, KV_RANK:], put_low)
    high = mm(own[:, KV_RANK:], put_high)
    for t in range(4):
        lat[me, 128:CHUNK, 128 * t : 128 * t + 128] = (
            low[32 * t : 32 * t + 16] + high[32 * t + 16 : 32 * t + 32]
        ).astype(BF)

    pl.semaphore_wait(barrier, len(z_partners) + chips)

    my_slice = pl.ds(pl.multiple_of((core * chips + rep // 2) * slice_rows, 16), slice_rows)
    far_w = pltpu.make_async_remote_copy(
        w_hbm.at[my_slice, :], wbuf.at[1, my_slice, :], w1_s, w1_r, device_id={"seq": at(8)}, device_id_type=MESH
    )
    far_w.start()

    def ring_copy(held, way, step, rows, j):
        ref = lat.at[held, rows]
        return pltpu.make_async_remote_copy(
            ref, ref, ring_s.at[way, step, j], ring_r.at[way, step, j],
            device_id={"seq": at(1) if way == 0 else at(-1)}, device_id_type=MESH,
        )

    def ring(way, step, rows, j):
        return ring_copy(at(-step) if way == 0 else at(step), way, step, rows, j)

    def ring_in(way, step, rows, j):
        return ring_copy(at(-step - 1) if way == 0 else at(step + 1), way, step, rows, j)

    subs = [pl.ds(j * SUB, SUB) for j in range(3)]
    halves = [pl.ds(0, 80), pl.ds(80, 64)]
    for j in range(3):
        for way in (0, 1):
            ring(way, 0, subs[j], j).start()

    def q_copy(shard, d):
        z = at(d)
        head_shard = lax.rem(z + 8 * shard, SEQ)
        slot = -d - first_of(z)
        return pltpu.make_async_remote_copy(
            q_hbm.at[:, pl.ds(pl.multiple_of(head_shard * (HEADS_HERE * QW), 128), HEADS_HERE * QW)],
            qbuf.at[shard, pl.ds(pl.multiple_of(slot * NEW, 16), NEW), :],
            q_s.at[shard, lax.rem(d + SEQ, SEQ)], q_r.at[shard, lax.rem(d + SEQ, SEQ)],
            device_id={"seq": z}, device_id_type=MESH,
        )

    def q_own(shard):
        head_shard = lax.rem(me + 8 * shard, SEQ)
        slot = -first_of(me)
        return pltpu.make_async_copy(
            q_hbm.at[:, pl.ds(pl.multiple_of(head_shard * (HEADS_HERE * QW), 128), HEADS_HERE * QW)],
            qbuf.at[shard, pl.ds(pl.multiple_of(slot * NEW, 16), NEW), :], loc_q.at[shard],
        )

    q_farthest = 8 * odd - 4
    q_away = (1, -1, 2, -2, 3, -3, q_farthest)

    def nth(i):
        return (1 - 2 * lax.rem(i, 2)) * (i // 2 + 1)

    def q_wait(shard):
        q_own(shard).wait()
        for d in q_away:
            q_copy(shard, d).wait_recv()

    q_own(0).start()
    q_own(1).start()
    q_copy(0, q_farthest).start()

    def w_copy(d):
        return pltpu.make_async_remote_copy(
            wbuf.at[1, my_slice, :], wbuf.at[1, my_slice, :], w2_s.at[d], w2_r.at[d],
            device_id={"rep": lax.rem(rep + 2 * d, reps)}, device_id_type=MESH,
        )

    my_half = pl.ds(pl.multiple_of(core * (KV_RANK // 2), 16), KV_RANK // 2)
    half_w = pltpu.make_async_remote_copy(
        wbuf.at[1, my_half, :], wbuf.at[1, my_half, :], w3_s, w3_r, device_id={"rep": sibling}, device_id_type=MESH
    )

    def spread(d, c):
        w_copy(d).start()
        return c

    def w_wait(d, c):
        w_copy(d).wait_recv()
        return c

    pr = lax.broadcasted_iota(jnp.int32, (2 * QW, 512), 0)
    pc = lax.broadcasted_iota(jnp.int32, (2 * QW, 512), 1)
    want = jnp.where(pc < 256, jnp.where(pc < QW, pc, -1), jnp.where(pc < 256 + QW, pc - 256 + QW, -1))
    perm[...] = jnp.where(pr == want, 1.0, 0.0).astype(BF)
    sr = lax.broadcasted_iota(jnp.int32, (128, 256), 0)
    sc = lax.broadcasted_iota(jnp.int32, (128, 256), 1)
    want = jnp.where(sc < 128, jnp.where(sc < ROPE, sc, -1), jnp.where(sc < 128 + ROPE, sc - 128 + ROPE, -1))
    sel[...] = jnp.where(sr == want, 1.0, 0.0).astype(BF)
    row = lax.broadcasted_iota(jnp.int32, (ROWS, SEQ * NEW), 0)
    col = lax.broadcasted_iota(jnp.int32, (ROWS, SEQ * NEW), 1)
    token = row + (me + first_of(me) + SEQ) * NEW
    token = jnp.where(token >= 2 * SEQ * NEW, token - 2 * SEQ * NEW, jnp.where(token >= SEQ * NEW, token - SEQ * NEW, token))
    bias[...] = jnp.where(col <= token, 0.0, -jnp.inf)

    def put(ref, head, src, val):
        ref[head, pl.ds(pl.multiple_of(src * PRE, 16), PRE), :] = val[0:PRE]
        ref[head, pl.ds(pl.multiple_of(PRE_ALL + src * NEW, 16), NEW), :] = val[PRE:]

    def project(shard, srcs):
        x = [lat[s, 0:128, :] for s in srcs]
        x = x[0] if len(x) == 1 else jnp.concatenate(x, axis=0)
        for h in range(HEADS_HERE):
            kv = mm(x, wbuf[shard, :, SPAN * h : SPAN * h + SPAN]).astype(BF)
            for n, s in enumerate(srcs):
                put(kbuf, shard * HEADS_HERE + h, s, kv[128 * n : 128 * n + 128, 0:NOPE])
                put(vbuf, shard * HEADS_HERE + h, s, kv[128 * n : 128 * n + 128, NOPE:])

    def unpack_rope(src):
        for t in range(4):
            pair = mm(lat[src, 128:CHUNK, 128 * t : 128 * t + 128], sel[...]).astype(BF)
            ropes[pl.ds(pl.multiple_of(src * PRE + 32 * t, 16), 16), :] = pair[:, 0:128]
            high = src * PRE + 32 * t + 16 if t < 3 else PRE_ALL + src * NEW
            ropes[pl.ds(pl.multiple_of(high, 16), 16), :] = pair[:, 128:]

    def both(i):
        return at(-i), at(i)

    def ring_step(step, c):
        for j in range(3):
            for way in (0, 1):
                ring_in(way, step - 1, subs[j], j).wait_recv()
                ring(way, step, subs[j], j).start()
            if j == 0:
                q_copy(0, nth(step - 1)).start()

                @pl.when(step == 1)
                def _():
                    own_w.wait()

            if j == 1:
                project(0, both(step - 1))
                for s in both(step - 1):
                    unpack_rope(s)

        @pl.when(step == 1)
        def _():
            far_w.wait_recv()
            lax.fori_loop(1, chips, spread, 0)

        @pl.when(step == HALF_AT)
        def _():
            lax.fori_loop(1, chips, w_wait, 0)
            half_w.start()

        @pl.when(step >= Q1_FROM)
        def _():
            q_copy(1, nth(step - Q1_FROM)).start()

        @pl.when(step >= FAR_AT)
        def _():
            @pl.when(step == FAR_AT)
            def _():
                half_w.wait_recv()

            def unit(i, c):
                project(1, both((step - FAR_AT) * FAR_UNITS + i))
                return c

            lax.fori_loop(0, FAR_UNITS, unit, 0)

        return c

    lax.fori_loop(1, 7, ring_step, 0)
    for j in range(3):
        for way in (0, 1):
            ring_in(way, 6, subs[j], j).wait_recv()
        if j > 0:
            ring(j - 1, 7, halves[j - 1], 0).start()
    for i in range(7 - Q1_FROM, 6):
        q_copy(1, nth(i)).start()
    q_copy(1, q_farthest).start()

    def rest(i, c):
        project(lax.rem(i, 2), both(6 + i // 2))
        return c

    lax.fori_loop(0, 4, rest, 0)
    for i in (6, 7):
        for s in both(i):
            unpack_rope(s)
    for way in (0, 1):
        ring_in(way, 7, halves[way], 0).wait_recv()

    def last(shard, c):
        project(shard, (at(8),))
        return c

    lax.fori_loop(0, 2, last, 0)
    unpack_rope(at(8))

    factor = math.log2(math.e) / math.sqrt(QW)
    o_away = (1, -1, 2, -2, 3, -3, 4 - 8 * odd)

    def o_place(shard, pair, slot):
        cols = lax.rem(me + 8 * shard, SEQ) * (HEADS_HERE * VDIM) + pair * (2 * VDIM)
        return (
            obuf.at[shard * 4 + pair, pl.ds(pl.multiple_of(slot * NEW, 16), NEW), :],
            out_hbm.at[:, pl.ds(pl.multiple_of(cols, 128), 2 * VDIM)],
        )

    def o_copy(shard, pair, d):
        src, dst = o_place(shard, pair, d - first_of(me))
        return pltpu.make_async_remote_copy(
            src, dst, o_s.at[shard, pair, lax.rem(d + SEQ, SEQ)], o_r.at[shard, pair, lax.rem(d + SEQ, SEQ)],
            device_id={"seq": at(d)}, device_id_type=MESH,
        )

    def o_own(shard, pair):
        src, dst = o_place(shard, pair, -first_of(me))
        return pltpu.make_async_copy(src, dst, loc_o.at[shard, pair])

    def attend(i, c):
        shard, pair = i // 4, lax.rem(i, 4)

        @pl.when(i == 0)
        def _():
            q_wait(0)

        @pl.when(i == 4)
        def _():
            q_wait(1)

        qp = qbuf[shard, :, pl.ds(pl.multiple_of(pair * (2 * QW), 128), 2 * QW)]
        qp = mm(qp, perm[...]).astype(BF)
        for n in range(2):
            head = shard * HEADS_HERE + 2 * pair + n
            keys = jnp.concatenate([kbuf[head], ropes[...]], axis=1)
            s = mm_t(qp[:, 256 * n : 256 * n + 256], keys)
            s = jnp.concatenate([s[:, 0:PRE_ALL], s[:, PRE_ALL:] + bias[...]], axis=1)
            top = jnp.max(s, axis=1, keepdims=True)
            e = jnp.exp2((s - top) * factor)
            total = jnp.sum(e, axis=1, keepdims=True)
            o = mm(e.astype(BF), vbuf[head]) / total
            obuf[i, :, VDIM * n : VDIM * n + VDIM] = o.astype(BF)
        o_own(shard, pair).start()
        for d in o_away:
            o_copy(shard, pair, d).start()
        return c

    lax.fori_loop(0, 8, attend, 0)

    def o_wait(i, c):
        shard, pair = i // 4, lax.rem(i, 4)
        o_own(shard, pair).wait()
        for d in o_away:
            o_copy(shard, pair, d).wait_send()
            o_copy(shard, pair, d).wait_recv()
        return c

    lax.fori_loop(0, 8, o_wait, 0)
    for shard in (0, 1):
        for d in q_away:
            q_copy(shard, d).wait_send()
    far_w.wait_send()

    def w_sent(d, c):
        w_copy(d).wait_send()
        return c

    lax.fori_loop(1, chips, w_sent, 0)
    half_w.wait_send()

    def ring_sent(step, c):
        for way in (0, 1):
            for j in range(3):
                ring(way, step, subs[j], j).wait_send()
        return c

    lax.fori_loop(0, 7, ring_sent, 0)
    for way in (0, 1):
        ring(way, 7, halves[way], 0).wait_send()


def body(queries, stretch_latent, prefix_latent, kv_up_weight):
    reps = lax.axis_size("rep")
    dma = pltpu.SemaphoreType.DMA
    hbm = pl.BlockSpec(memory_space=pltpu.HBM)
    return pl.pallas_call(
        functools.partial(kernel, reps),
        out_shape=jax.ShapeDtypeStruct((NEW, SEQ * HEADS_HERE * VDIM), BF),
        in_specs=[hbm] * 4,
        out_specs=pl.BlockSpec(memory_space=pl.ANY),
        scratch_shapes=[
            pltpu.VMEM((PRE + NEW, KV_RANK + ROPE), BF),
            pltpu.VMEM((SEQ, CHUNK, KV_RANK), BF),
            pltpu.VMEM((2, ROWS, HEADS_HERE * QW), BF),
            pltpu.VMEM((2, KV_RANK, HEADS_HERE * SPAN), BF),
            pltpu.VMEM((2 * HEADS_HERE, KEYS, NOPE), BF),
            pltpu.VMEM((2 * HEADS_HERE, KEYS, VDIM), BF),
            pltpu.VMEM((KEYS, 128), BF),
            pltpu.VMEM((HEADS_HERE, ROWS, 2 * VDIM), BF),
            pltpu.VMEM((2 * QW, 512), BF),
            pltpu.VMEM((128, 256), BF),
            pltpu.VMEM((ROWS, SEQ * NEW), F32),
            dma((2, 8, 3)), dma((2, 8, 3)),
            dma((2, SEQ)), dma((2, SEQ)),
            dma((2, 4, SEQ)), dma((2, 4, SEQ)),
            dma, dma, dma((reps // 2,)), dma((reps // 2,)), dma, dma,
            dma, dma((2,)), dma((2,)), dma((2, 4)),
        ],
        compiler_params=pltpu.CompilerParams(
            collective_id=0, has_side_effects=True, vmem_limit_bytes=60 * 1024 * 1024
        ),
        cost_estimate=pl.CostEstimate(flops=13_000_000_000, bytes_accessed=8_000_000, transcendentals=4_200_000),
    )(prefix_latent, stretch_latent, queries, kv_up_weight)


def solution(mesh):
    in_specs = (
        P(("rep", "seq"), None),
        P(("rep", "seq"), None),
        P(("rep", "seq"), None),
        P(None, "seq"),
    )
    out_specs = P(("rep", "seq"), None)
    return jax.shard_map(body, mesh=mesh, in_specs=in_specs, out_specs=out_specs, check_vma=False)
```

time: 101 us -> 87 us (0.86)
  the two profiles are of different devices: /device:TPU:16 before, /device:TPU:32 now
where the time goes in v2:
time: 87 us; the launch traced here: 86.8 us
  Pallas kernels  84.9 us (98%)
  local copies, waits for them, and re-layouts  1.87 us (2%)
    pallas_call x1, Pallas kernels, body(): pl.pallas_call(functools.partial(kernel, reps), out_shape=jax.ShapeDtypeS...  84.9 us
    unnamed x1, local copies, waits for them, and re-layouts  1.87 us

profile of v2, /device:TPU:32, one launch (start us, length us, event | category | flops | bytes accessed | tf_op | source)
XLA Modules:
  0.0 86.8 jit_solution(12507180581070066640)
XLA Ops:
  0.0 84.9 %shard_map.46 = bf16[16,16384]{1,0:T(8,128)(2,1)} custom-call(bf16[112,576]{1,0:T(8,128)(2,1)} %prefix_hbm.1, bf16[16,576]{1,0:T(8,128)(2,1)} %stretch_hbm.1, bf16[16,24576]{1,0:T(8,128)(2,1)} %q_hbm.1, bf16[512,2048]{1,0:T(8,128)(2,1)} %w_hbm.1), custom_call_target="tpu_custom_call" | custom-call | flops 12999999488 | bytes 8000000 | tf_op jit(solution)/shard_map/pallas_call | solution.py:372
  84.9 1.9 %copy.6 = bf16[16,16384]{1,0:T(8,128)(2,1)} copy(bf16[16,16384]{1,0:T(8,128)(2,1)} %shard_map.46) | data formatting | bytes 1048576

commit v3 on v2

--- a/solution.py
+++ b/solution.py
@@ -58,25 +58,30 @@
         return lax.rem(me + d + 2 * SEQ, SEQ)
 
     def first_of(z):
-        return -3 - lax.rem(z, 2)
-
-    barrier = pltpu.get_barrier_semaphore()
-    z_partners = (1, -1, 2, -2, 3, -3, 4, -4, 8)
-    for d in z_partners:
-        pl.semaphore_signal(barrier, inc=1, device_id={"seq": at(d)}, device_id_type=MESH)
-
-    def greet(d, c):
-        pl.semaphore_signal(barrier, inc=1, device_id={"rep": lax.rem(rep + 2 * d, reps)}, device_id_type=MESH)
-        return c
-
-    lax.fori_loop(1, chips, greet, 0)
-    pl.semaphore_signal(barrier, inc=1, device_id={"rep": sibling}, device_id_type=MESH)
+        return lax.rem(z, 2) - 4
+
+    def shard_of(z, shard):
+        return lax.rem(z + shard * (7 + 2 * lax.rem(z, 2)), SEQ)
 
     own_prefix = pltpu.make_async_copy(prefix_hbm, own.at[0:PRE, :], loc_x.at[0])
     own_stretch = pltpu.make_async_copy(stretch_hbm, own.at[PRE : PRE + NEW, :], loc_x.at[1])
     own_w = pltpu.make_async_copy(w_hbm, wbuf.at[0], loc_w)
     own_prefix.start()
     own_stretch.start()
+
+    barrier = pltpu.get_barrier_semaphore()
+    far = 7 - 14 * odd
+    z_partners = (1, -1, 2, -2, 3, -3, 4, -4, far)
+    for d in z_partners:
+        pl.semaphore_signal(barrier, inc=1, device_id={"seq": at(d)}, device_id_type=MESH)
+
+    def greet(d, c):
+        pl.semaphore_signal(barrier, inc=1, device_id={"rep": lax.rem(rep + 2 * d, reps)}, device_id_type=MESH)
+        return c
+
+    lax.fori_loop(1, chips, greet, 0)
+    pl.semaphore_signal(barrier, inc=1, device_id={"rep": sibling}, device_id_type=MESH)
+
     own_w.start()
     r64 = lax.broadcasted_iota(jnp.int32, (ROPE, 128), 0)
     c64 = lax.broadcasted_iota(jnp.int32, (ROPE, 128), 1)
@@ -85,18 +90,11 @@
     own_prefix.wait()
     own_stretch.wait()
     lat[me, 0:128, :] = own[:, 0:KV_RANK]
-    low = mm(own[:, KV_RANK:], put_low)
-    high = mm(own[:, KV_RANK:], put_high)
-    for t in range(4):
-        lat[me, 128:CHUNK, 128 * t : 128 * t + 128] = (
-            low[32 * t : 32 * t + 16] + high[32 * t + 16 : 32 * t + 32]
-        ).astype(BF)
-
     pl.semaphore_wait(barrier, len(z_partners) + chips)
 
     my_slice = pl.ds(pl.multiple_of((core * chips + rep // 2) * slice_rows, 16), slice_rows)
     far_w = pltpu.make_async_remote_copy(
-        w_hbm.at[my_slice, :], wbuf.at[1, my_slice, :], w1_s, w1_r, device_id={"seq": at(8)}, device_id_type=MESH
+        w_hbm.at[my_slice, :], wbuf.at[1, my_slice, :], w1_s, w1_r, device_id={"seq": at(far)}, device_id_type=MESH
     )
     far_w.start()
 
@@ -116,12 +114,19 @@
     subs = [pl.ds(j * SUB, SUB) for j in range(3)]
     halves = [pl.ds(0, 80), pl.ds(80, 64)]
     for j in range(3):
+        if j == 2:
+            low = mm(own[:, KV_RANK:], put_low)
+            high = mm(own[:, KV_RANK:], put_high)
+            for t in range(4):
+                lat[me, 128:CHUNK, 128 * t : 128 * t + 128] = (
+                    low[32 * t : 32 * t + 16] + high[32 * t + 16 : 32 * t + 32]
+                ).astype(BF)
         for way in (0, 1):
             ring(way, 0, subs[j], j).start()
 
     def q_copy(shard, d):
         z = at(d)
-        head_shard = lax.rem(z + 8 * shard, SEQ)
+        head_shard = shard_of(z, shard)
         slot = -d - first_of(z)
         return pltpu.make_async_remote_copy(
             q_hbm.at[:, pl.ds(pl.multiple_of(head_shard * (HEADS_HERE * QW), 128), HEADS_HERE * QW)],
@@ -131,14 +136,14 @@
         )
 
     def q_own(shard):
-        head_shard = lax.rem(me + 8 * shard, SEQ)
+        head_shard = shard_of(me, shard)
         slot = -first_of(me)
         return pltpu.make_async_copy(
             q_hbm.at[:, pl.ds(pl.multiple_of(head_shard * (HEADS_HERE * QW), 128), HEADS_HERE * QW)],
             qbuf.at[shard, pl.ds(pl.multiple_of(slot * NEW, 16), NEW), :], loc_q.at[shard],
         )
 
-    q_farthest = 8 * odd - 4
+    q_farthest = 4 - 8 * odd
     q_away = (1, -1, 2, -2, 3, -3, q_farthest)
 
     def nth(i):
@@ -283,10 +288,10 @@
     unpack_rope(at(8))
 
     factor = math.log2(math.e) / math.sqrt(QW)
-    o_away = (1, -1, 2, -2, 3, -3, 4 - 8 * odd)
+    o_away = (1, -1, 2, -2, 3, -3, 8 * odd - 4)
 
     def o_place(shard, pair, slot):
-        cols = lax.rem(me + 8 * shard, SEQ) * (HEADS_HERE * VDIM) + pair * (2 * VDIM)
+        cols = shard_of(me, shard) * (HEADS_HERE * VDIM) + pair * (2 * VDIM)
         return (
             obuf.at[shard * 4 + pair, pl.ds(pl.multiple_of(slot * NEW, 16), NEW), :],
             out_hbm.at[:, pl.ds(pl.multiple_of(cols, 128), 2 * VDIM)],
@@ -316,10 +321,14 @@
 
         qp = qbuf[shard, :, pl.ds(pl.multiple_of(pair * (2 * QW), 128), 2 * QW)]
         qp = mm(qp, perm[...]).astype(BF)
+        ss = []
         for n in range(2):
             head = shard * HEADS_HERE + 2 * pair + n
             keys = jnp.concatenate([kbuf[head], ropes[...]], axis=1)
-            s = mm_t(qp[:, 256 * n : 256 * n + 256], keys)
+            ss.append(mm_t(qp[:, 256 * n : 256 * n + 256], keys))
+        for n in range(2):
+            head = shard * HEADS_HERE + 2 * pair + n
+            s = ss[n]
             s = jnp.concatenate([s[:, 0:PRE_ALL], s[:, PRE_ALL:] + bias[...]], axis=1)
             top = jnp.max(s, axis=1, keepdims=True)
             e = jnp.exp2((s - top) * factor)

time: 87 us -> 85.4 us (0.982)
  Pallas kernels: 84.9 us -> 83.4 us
    pallas_call x1, Pallas kernels: 84.9 us -> 83.4 us  [body(): pl.pallas_call(functools.partial(kernel, reps), out_shape=jax.ShapeDtypeS...]
where the time goes in v3:
time: 85.4 us; the launch traced here: 85.2 us
  Pallas kernels  83.4 us (98%)
  local copies, waits for them, and re-layouts  1.87 us (2%)
    pallas_call x1, Pallas kernels, body(): pl.pallas_call(functools.partial(kernel, reps), out_shape=jax.ShapeDtypeS...  83.4 us
    unnamed x1, local copies, waits for them, and re-layouts  1.87 us

profile of v3, /device:TPU:32, one launch (start us, length us, event | category | flops | bytes accessed | tf_op | source)
XLA Modules:
  0.0 85.2 jit_solution(8284409338818302444)
XLA Ops:
  0.0 83.4 %shard_map.46 = bf16[16,16384]{1,0:T(8,128)(2,1)} custom-call(bf16[112,576]{1,0:T(8,128)(2,1)} %prefix_hbm.1, bf16[16,576]{1,0:T(8,128)(2,1)} %stretch_hbm.1, bf16[16,24576]{1,0:T(8,128)(2,1)} %q_hbm.1, bf16[512,2048]{1,0:T(8,128)(2,1)} %w_hbm.1), custom_call_target="tpu_custom_call" | custom-call | flops 12999999488 | bytes 8000000 | tf_op jit(solution)/shard_map/pallas_call | solution.py:381
  83.4 1.9 %copy.6 = bf16[16,16384]{1,0:T(8,128)(2,1)} copy(bf16[16,16384]{1,0:T(8,128)(2,1)} %shard_map.46) | data formatting | bytes 1048576
